TPU v7x, 512 devices: a whole 4x4x16 slice. The times are simulated.
512 devices in a mesh: dp: 64 (over z_hi, x, y, core), head: 8 (over z_lo).
Axes of the slice: x: 4, y: 4, z: 16 (z_hi: 2, z_lo: 8; z = z_hi * 8 + z_lo), core: 2. Of those that a mesh axis runs over, the one named last changes fastest.
Arguments:
- queries: bfloat16 [65536, 8192], P('dp', 'head'), may hold values from -48 to 48
- keys: bfloat16 [65536, 1024], P('dp', 'head'), may hold values from -4 to 4
- values: bfloat16 [65536, 1024], P('dp', 'head'), may hold values from -6 to 6
- segments: int32 [64, 1024], P('dp'), may hold values from 0 to 1023, as said below
Outputs:
- attended: bfloat16 [65536, 8192], P(('dp', 'head'))
Inputs may be any that keep to these rules, and one draw needn't show every extreme that they name: `segments`: in every row the ids start at 0 and never fall; a document is a run of equal ids. A replica whose index has an even number of one bits starts all its documents within its first 256 tokens; any other replica starts a document at every multiple of 256. Some replica consists of 1024 documents of one token each.
All inputs are finite; a program needn't handle non-finite values.
Results may differ from a plain program's by a relative error of at most 0.0021.
Values may be sent and summed in bfloat16 or wider, within the bound.
A program may use at most 128 MiB of HBM per device.

v0:
```python
import jax
import jax.numpy as jnp
from jax import lax
from jax.experimental import pallas as pl
from jax.experimental.pallas import tpu as pltpu
from jax.sharding import PartitionSpec as P

HEADS = 8
WIDTH = 128
GROUP = 8
BLK = 256
PIECE = 32
MESH = pl.DeviceIdType.MESH
LOG2E = 1.4426950408889634


def xor(a, b):
    total = 0
    for bit in (1, 2, 4):
        total = total + bit * (((a // bit) % 2 + (b // bit) % 2) % 2)
    return total


def step_offset(step):
    even = 1 - step % 2
    return even * (4 + step // 2) + (1 - even) * (((step + 1) // 2) % 4)


def kernel(
    q_hbm, k_hbm, v_hbm, seg_ref, out_ref,
    q_ref, k_ref, v_ref, seg_col, sent, q_sem, kv_sem, send_sem, recv_sem,
):
    tokens, width = q_ref.shape
    chunk = tokens // HEADS
    pieces = chunk // PIECE
    scale = WIDTH**-0.5 * LOG2E
    me = lax.axis_index("head")
    replica = lax.axis_index("dp")
    ones = 0
    for bit in range(16):
        ones = ones + (replica // 2**bit) % 2
    light = ones % 2

    def q_copy(step):
        rows = pl.ds(pl.multiple_of(xor(me, step_offset(step)) * chunk, chunk), chunk)
        return pltpu.make_async_copy(q_hbm.at[rows], q_ref.at[rows], q_sem.at[step])

    k_copy = pltpu.make_async_copy(k_hbm, k_ref, kv_sem.at[0])
    v_copy = pltpu.make_async_copy(v_hbm, v_ref, kv_sem.at[1])
    barrier = pltpu.get_barrier_semaphore()
    for offset in range(1, HEADS):
        pl.semaphore_signal(
            barrier, inc=1, device_id={"head": xor(me, offset)}, device_id_type=MESH
        )
    q_copy(0).start()
    k_copy.start()
    v_copy.start()
    for step in range(1, HEADS):
        q_copy(step).start()
    for part in range(tokens // 128):
        row = seg_ref[0:1, part * 128 : (part + 1) * 128]
        seg_col[part * 128 : (part + 1) * 128, :] = jnp.broadcast_to(row, (128, 128)).T
    k_copy.wait()
    v_copy.wait()
    pl.semaphore_wait(barrier, HEADS - 1)

    def piece_copy(step, piece):
        offset = step_offset(step)
        partner = xor(me, offset)
        source = pl.ds(pl.multiple_of(partner * chunk + piece * PIECE, PIECE), PIECE)
        return pltpu.make_async_remote_copy(
            src_ref=sent.at[source],
            dst_ref=out_ref.at[
                pl.ds(pl.multiple_of(piece * PIECE, PIECE), PIECE),
                pl.ds(pl.multiple_of(me * width, width), width),
            ],
            send_sem=send_sem.at[step, piece],
            recv_sem=recv_sem.at[step, piece],
            device_id={"head": partner},
            device_id_type=MESH,
        )

    def attend(first, key_first, blocks):
        keys = blocks * BLK
        rows = pl.ds(first, PIECE)
        window = pl.ds(key_first, keys)
        queries = jnp.concatenate(
            [q_ref[rows, g * WIDTH : (g + 1) * WIDTH] for g in range(GROUP)], axis=0
        )
        scores = lax.dot_general(
            queries, k_ref[window, :], (((1,), (1,)), ((), ())),
            preferred_element_type=jnp.float32,
        )
        own = seg_col[rows, :]
        own = jnp.concatenate([own] * (keys // 128), axis=1)
        key_seg = seg_ref[0:1, window]
        key_at = key_first + lax.broadcasted_iota(jnp.int32, (PIECE, keys), 1)
        own_at = first + lax.broadcasted_iota(jnp.int32, (PIECE, keys), 0)
        allowed = (own == key_seg) & (key_at <= own_at)
        bias = jnp.where(allowed, 0.0, -jnp.inf)
        scores = scores.reshape(GROUP, PIECE, keys) + bias[None]
        row_max = jnp.max(scores, axis=-1, keepdims=True)
        weights = jnp.exp2((scores - row_max) * scale)
        total = jnp.sum(weights, axis=-1, keepdims=True)
        mixed = jnp.dot(
            weights.astype(jnp.bfloat16).reshape(GROUP * PIECE, keys), v_ref[window, :],
            preferred_element_type=jnp.float32,
        )
        mixed = mixed.reshape(GROUP, PIECE, WIDTH) / total
        for g in range(GROUP):
            sent[rows, g * WIDTH : (g + 1) * WIDTH] = mixed[g].astype(jnp.bfloat16)

    def one_step(step, carry):
        partner = xor(me, step_offset(step))
        q_copy(step).wait()
        block = partner // (BLK // chunk)
        blocks = light + (1 - light) * (block + 1)
        key_first = pl.multiple_of(light * block * BLK, BLK)

        def one_piece(piece, inner):
            first = pl.multiple_of(partner * chunk + piece * PIECE, PIECE)
            for count in range(1, tokens // BLK + 1):

                @pl.when(blocks == count)
                def _(count=count):
                    attend(first, key_first if count == 1 else 0, count)

            @pl.when(step < HEADS - 1)
            def _():
                piece_copy(step, piece).start()

            return inner

        return lax.fori_loop(0, pieces, one_piece, carry)

    lax.fori_loop(0, HEADS, one_step, 0)
    mine = pl.ds(pl.multiple_of(me * chunk, chunk), chunk)
    home = pltpu.make_async_copy(
        sent.at[mine],
        out_ref.at[:, pl.ds(pl.multiple_of(me * width, width), width)],
        kv_sem.at[0],
    )
    home.start()
    home.wait()

    def finish(step, carry):
        def one_piece(piece, inner):
            copy = piece_copy(step, piece)
            copy.wait_send()
            copy.wait_recv()
            return inner

        return lax.fori_loop(0, pieces, one_piece, carry)

    lax.fori_loop(0, HEADS - 1, finish, 0)


def on_device(queries, keys, values, segments):
    tokens, width = queries.shape
    chunk = tokens // HEADS
    pieces = chunk // PIECE
    return pl.pallas_call(
        kernel,
        out_shape=jax.ShapeDtypeStruct((chunk, HEADS * width), queries.dtype),
        in_specs=[pl.BlockSpec(memory_space=pl.ANY)] * 3
        + [pl.BlockSpec(memory_space=pltpu.VMEM)],
        out_specs=pl.BlockSpec(memory_space=pl.ANY),
        scratch_shapes=[
            pltpu.VMEM(queries.shape, queries.dtype),
            pltpu.VMEM(keys.shape, keys.dtype),
            pltpu.VMEM(values.shape, values.dtype),
            pltpu.VMEM((tokens, 128), jnp.int32),
            pltpu.VMEM(queries.shape, queries.dtype),
            pltpu.SemaphoreType.DMA((HEADS,)),
            pltpu.SemaphoreType.DMA((2,)),
            pltpu.SemaphoreType.DMA((HEADS - 1, pieces)),
            pltpu.SemaphoreType.DMA((HEADS - 1, pieces)),
        ],
        compiler_params=pltpu.CompilerParams(
            collective_id=0, has_side_effects=True, vmem_limit_bytes=40 * 2**20
        ),
        cost_estimate=pl.CostEstimate(
            flops=4 * tokens * width * tokens, bytes_accessed=5 * 2**20,
            transcendentals=tokens * GROUP * tokens,
        ),
    )(queries, keys, values, segments)


def solution(mesh):
    placed = (P("dp", "head"), P("dp", "head"), P("dp", "head"), P("dp", None))
    return jax.shard_map(
        on_device, mesh=mesh, in_specs=placed, out_specs=P(("dp", "head"), None), check_vma=False
    )
```

profile of v0, /device:TPU:29, one launch (start us, length us, event | category | flops | bytes accessed | tf_op | source)
XLA Modules:
  0.0 106.2 jit_solution(11006755323996637147)
XLA Ops:
  0.0 0.0 copy-start
  0.0 1.6 %copy-done = bf16[1024,1024]{1,0:T(8,128)(2,1)S(1)} copy-done((bf16[1024,1024]{1,0:T(8,128)(2,1)S(1)}, bf16[1024,1024]{1,0:T(8,128)(2,1)}, u32[]{:S(2)}) %copy-start) | copy-done | bytes 2097176
  1.6 0.0 copy-start.1
  1.6 0.9 copy-done.1
  2.5 0.0 copy-start.2
  2.5 0.9 copy-done.2
  3.5 0.0 copy-start.3
  3.5 0.7 copy-done.3
  4.2 100.7 %shard_map.46 = bf16[128,8192]{1,0:T(8,128)(2,1)S(1)} custom-call(bf16[1024,1024]{1,0:T(8,128)(2,1)S(1)} %copy-done, bf16[1024,128]{1,0:T(8,128)(2,1)S(1)} %copy-done.1, bf16[1024,128]{1,0:T(8,128)(2,1)S(1)} %copy-done.2, s32[1,1024]{1,0:T(1,128)S(1)} %copy-done.3), custom_call_target="tpu_custom_call" | custom-call | flops 4294967296 | bytes 5242880 | tf_op jit(solution)/shard_map/pallas_call | solution.py:162
  104.9 1.3 %copy.6 = bf16[128,8192]{1,0:T(8,128)(2,1)} copy(bf16[128,8192]{1,0:T(8,128)(2,1)S(1)} %shard_map.46) | data formatting | bytes 4194304
Async XLA Ops:
  0.0 1.6 %copy-start = (bf16[1024,1024]{1,0:T(8,128)(2,1)S(1)}, bf16[1024,1024]{1,0:T(8,128)(2,1)}, u32[]{:S(2)}) copy-start(bf16[1024,1024]{1,0:T(8,128)(2,1)} %q_hbm.1) | copy-start | bytes 6291460
  1.6 0.9 copy-start.1
  2.5 0.9 copy-start.2
  3.5 0.7 copy-start.3
where the time goes:
time: 106 us
  Pallas kernels  101 us (95%)
  local copies, waits for them, and re-layouts  5.5 us (5%)
    pallas_call x1, Pallas kernels, on_device(): pl.pallas_call(kernel, out_shape=jax.ShapeDtypeStruct((chunk, HEADS * wid...  101 us
    unnamed x9, local copies, waits for them, and re-layouts  5.5 us

commit v1 on v0

--- a/solution.py
+++ b/solution.py
@@ -21,18 +21,14 @@
     return total
 
 
-def step_offset(step):
-    even = 1 - step % 2
-    return even * (4 + step // 2) + (1 - even) * (((step + 1) // 2) % 4)
-
-
 def kernel(
-    q_hbm, k_hbm, v_hbm, seg_ref, out_ref,
-    q_ref, k_ref, v_ref, seg_col, sent, q_sem, kv_sem, send_sem, recv_sem,
+    q_hbm, k_hbm, v_hbm, seg_hbm, out_ref,
+    q_ref, k_ref, v_ref, seg_ref, seg_col, sent, q_sem, in_sem, send_sem, recv_sem, ready,
 ):
     tokens, width = q_ref.shape
     chunk = tokens // HEADS
     pieces = chunk // PIECE
+    half = HEADS // 2
     scale = WIDTH**-0.5 * LOG2E
     me = lax.axis_index("head")
     replica = lax.axis_index("dp")
@@ -40,33 +36,85 @@
     for bit in range(16):
         ones = ones + (replica // 2**bit) % 2
     light = ones % 2
+    flip = replica // (lax.axis_size("dp") // 2)
+    place = me + flip * (HEADS - 1 - 2 * me)
+    late = place // half
+
+    def device(at):
+        return at + flip * (HEADS - 1 - 2 * at)
+
+    def target(step):
+        last = step // (HEADS - 1)
+        odd = (step % 2) * (1 - last)
+        across = odd + 1 - (step + HEADS - 2) // (HEADS - 1)
+        other = (step + 1) // 2 + half * (1 - late)
+        near = half * late + xor(place % half, (step // 2) * (1 - last))
+        return across * other + (1 - across) * near
 
     def q_copy(step):
-        rows = pl.ds(pl.multiple_of(xor(me, step_offset(step)) * chunk, chunk), chunk)
+        rows = pl.ds(pl.multiple_of(device(target(step)) * chunk, chunk), chunk)
         return pltpu.make_async_copy(q_hbm.at[rows], q_ref.at[rows], q_sem.at[step])
 
-    k_copy = pltpu.make_async_copy(k_hbm, k_ref, kv_sem.at[0])
-    v_copy = pltpu.make_async_copy(v_hbm, v_ref, kv_sem.at[1])
+    def greet(at, semaphore):
+        pl.semaphore_signal(
+            semaphore, inc=1, device_id={"head": device(at)}, device_id_type=MESH
+        )
+
     barrier = pltpu.get_barrier_semaphore()
-    for offset in range(1, HEADS):
-        pl.semaphore_signal(
-            barrier, inc=1, device_id={"head": xor(me, offset)}, device_id_type=MESH
-        )
+
+    @pl.when(late == 0)
+    def _():
+        for at in range(half, HEADS):
+            greet(at, barrier)
+
+    @pl.when(place == half)
+    def _():
+        for at in range(half):
+            greet(at, barrier)
+
+    seg_copy = pltpu.make_async_copy(seg_hbm, seg_ref, in_sem.at[2])
+    k_copy = pltpu.make_async_copy(k_hbm, k_ref, in_sem.at[0])
+    v_copy = pltpu.make_async_copy(v_hbm, v_ref, in_sem.at[1])
+    seg_copy.start()
     q_copy(0).start()
     k_copy.start()
     v_copy.start()
     for step in range(1, HEADS):
         q_copy(step).start()
+    seg_copy.wait()
     for part in range(tokens // 128):
         row = seg_ref[0:1, part * 128 : (part + 1) * 128]
         seg_col[part * 128 : (part + 1) * 128, :] = jnp.broadcast_to(row, (128, 128)).T
     k_copy.wait()
     v_copy.wait()
-    pl.semaphore_wait(barrier, HEADS - 1)
+
+    @pl.when(late == 0)
+    def _():
+        pl.semaphore_wait(barrier, 1)
+
+    @pl.when(late == 1)
+    def _():
+        pl.semaphore_wait(barrier, half)
+        for at in range(half):
+            greet(at, ready.at[place - half])
+
+    def admit(step):
+        @pl.when(step == 2)
+        def _():
+            pl.semaphore_wait(ready.at[0], 1)
+
+        @pl.when((late == 0) & (step % 2 == 1) & (step < HEADS - 1))
+        def _():
+            pl.semaphore_wait(ready.at[(step + 1) // 2], 1)
+
+        @pl.when((place == half - 1) & (step == HEADS - 3))
+        def _():
+            for at in range(half, HEADS):
+                greet(at, ready.at[0])
 
     def piece_copy(step, piece):
-        offset = step_offset(step)
-        partner = xor(me, offset)
+        partner = device(target(step))
+        link = xor(me, partner) - 1
         source = pl.ds(pl.multiple_of(partner * chunk + piece * PIECE, PIECE), PIECE)
         return pltpu.make_async_remote_copy(
             src_ref=sent.at[source],
@@ -74,8 +122,8 @@
                 pl.ds(pl.multiple_of(piece * PIECE, PIECE), PIECE),
                 pl.ds(pl.multiple_of(me * width, width), width),
             ],
-            send_sem=send_sem.at[step, piece],
-            recv_sem=recv_sem.at[step, piece],
+            send_sem=send_sem.at[link, piece],
+            recv_sem=recv_sem.at[link, piece],
             device_id={"head": partner},
             device_id_type=MESH,
         )
@@ -111,8 +159,9 @@
             sent[rows, g * WIDTH : (g + 1) * WIDTH] = mixed[g].astype(jnp.bfloat16)
 
     def one_step(step, carry):
-        partner = xor(me, step_offset(step))
+        partner = device(target(step))
         q_copy(step).wait()
+        admit(step)
         block = partner // (BLK // chunk)
         blocks = light + (1 - light) * (block + 1)
         key_first = pl.multiple_of(light * block * BLK, BLK)
@@ -138,7 +187,7 @@
     home = pltpu.make_async_copy(
         sent.at[mine],
         out_ref.at[:, pl.ds(pl.multiple_of(me * width, width), width)],
-        kv_sem.at[0],
+        in_sem.at[0],
     )
     home.start()
     home.wait()
@@ -161,23 +210,24 @@
     pieces = chunk // PIECE
     return pl.pallas_call(
         kernel,
-        out_shape=jax.ShapeDtypeStruct((chunk, HEADS * width), queries.dtype),
-        in_specs=[pl.BlockSpec(memory_space=pl.ANY)] * 3
-        + [pl.BlockSpec(memory_space=pltpu.VMEM)],
-        out_specs=pl.BlockSpec(memory_space=pl.ANY),
+        out_shape=pltpu.VMEM((chunk, HEADS * width), queries.dtype),
+        in_specs=[pl.BlockSpec(memory_space=pl.ANY)] * 4,
+        out_specs=pl.BlockSpec(memory_space=pltpu.VMEM),
         scratch_shapes=[
             pltpu.VMEM(queries.shape, queries.dtype),
             pltpu.VMEM(keys.shape, keys.dtype),
             pltpu.VMEM(values.shape, values.dtype),
+            pltpu.VMEM(segments.shape, segments.dtype),
             pltpu.VMEM((tokens, 128), jnp.int32),
             pltpu.VMEM(queries.shape, queries.dtype),
             pltpu.SemaphoreType.DMA((HEADS,)),
-            pltpu.SemaphoreType.DMA((2,)),
+            pltpu.SemaphoreType.DMA((3,)),
             pltpu.SemaphoreType.DMA((HEADS - 1, pieces)),
             pltpu.SemaphoreType.DMA((HEADS - 1, pieces)),
+            pltpu.SemaphoreType.REGULAR((HEADS // 2,)),
         ],
         compiler_params=pltpu.CompilerParams(
-            collective_id=0, has_side_effects=True, vmem_limit_bytes=40 * 2**20
+            collective_id=0, has_side_effects=True, vmem_limit_bytes=60 * 2**20
         ),
         cost_estimate=pl.CostEstimate(
             flops=4 * tokens * width * tokens, bytes_accessed=5 * 2**20,

time: 106 us -> 102 us (0.962)
  the two profiles are of different devices: /device:TPU:29 before, /device:TPU:275 now
where the time goes in v1:
time: 102 us; the launch traced here: 101 us
  Pallas kernels  100 us (98%)
  local copies, waits for them, and re-layouts  1.32 us (1%)
    pallas_call x1, Pallas kernels, on_device(): pl.pallas_call(kernel, out_shape=pltpu.VMEM((chunk, HEADS * width), queri...  100 us

profile of v1, /device:TPU:275, one launch (start us, length us, event | category | flops | bytes accessed | tf_op | source)
XLA Modules:
  0.0 101.5 jit_solution(7868555244990018006)
XLA Ops:
  0.0 100.1 %shard_map.46 = bf16[128,8192]{1,0:T(8,128)(2,1)S(1)} custom-call(bf16[1024,1024]{1,0:T(8,128)(2,1)} %q_hbm.1, bf16[1024,128]{1,0:T(8,128)(2,1)} %k_hbm.1, bf16[1024,128]{1,0:T(8,128)(2,1)} %v_hbm.1, s32[1,1024]{1,0:T(1,128)} %seg_hbm.1), custom_call_target="tpu_custom_call" | custom-call | flops 4294967296 | bytes 5242880 | tf_op jit(solution)/shard_map/pallas_call | solution.py:211
  100.2 1.3 %copy.6 = bf16[128,8192]{1,0:T(8,128)(2,1)} copy(bf16[128,8192]{1,0:T(8,128)(2,1)S(1)} %shard_map.46) | data formatting | bytes 4194304

commit v2 on v1

--- a/solution.py
+++ b/solution.py
@@ -12,6 +12,12 @@
 PIECE = 32
 MESH = pl.DeviceIdType.MESH
 LOG2E = 1.4426950408889634
+PACKED = 3
+TOGETHER = (4, 2, 4)
+
+
+def keys_of(piece):
+    return (piece + 1) * PIECE
 
 
 def xor(a, b):
@@ -23,12 +29,14 @@
 
 def kernel(
     q_hbm, k_hbm, v_hbm, seg_hbm, out_ref,
-    q_ref, k_ref, v_ref, seg_ref, seg_col, sent, q_sem, in_sem, send_sem, recv_sem, ready,
+    q_ref, k_ref, v_ref, seg_ref, seg_col, sent, v_came, spread_0, spread_1, spread_2,
+    q_sem, in_sem, send_sem, recv_sem, v_send_sem, v_recv_sem, ready,
 ):
     tokens, width = q_ref.shape
     chunk = tokens // HEADS
     pieces = chunk // PIECE
     half = HEADS // 2
+    spread = (spread_0, spread_1, spread_2)
     scale = WIDTH**-0.5 * LOG2E
     me = lax.axis_index("head")
     replica = lax.axis_index("dp")
@@ -36,6 +44,12 @@
     for bit in range(16):
         ones = ones + (replica // 2**bit) % 2
     light = ones % 2
+
+    def narrow(at):
+        even = 1 - at % (BLK // chunk)
+        first = 1 - (at + HEADS - 1) // HEADS
+        return light * even + (1 - light) * first
+
     flip = replica // (lax.axis_size("dp") // 2)
     place = me + flip * (HEADS - 1 - 2 * me)
     late = place // half
@@ -85,6 +99,14 @@
     for part in range(tokens // 128):
         row = seg_ref[0:1, part * 128 : (part + 1) * 128]
         seg_col[part * 128 : (part + 1) * 128, :] = jnp.broadcast_to(row, (128, 128)).T
+    for piece in range(PACKED):
+        keys = keys_of(piece)
+        spread[piece][...] = jnp.zeros_like(spread[piece])
+        row = lax.broadcasted_iota(jnp.int32, (keys, WIDTH), 0)
+        column = lax.broadcasted_iota(jnp.int32, (keys, WIDTH), 1)
+        unit = jnp.where(row == column, 1.0, 0.0).astype(jnp.bfloat16)
+        for g in range(TOGETHER[piece]):
+            spread[piece][g * keys : (g + 1) * keys, g * WIDTH : (g + 1) * WIDTH] = unit
     k_copy.wait()
     v_copy.wait()
 
@@ -112,15 +134,15 @@
             for at in range(half, HEADS):
                 greet(at, ready.at[0])
 
-    def piece_copy(step, piece):
+    def piece_copy(step, piece, columns):
         partner = device(target(step))
         link = xor(me, partner) - 1
         source = pl.ds(pl.multiple_of(partner * chunk + piece * PIECE, PIECE), PIECE)
         return pltpu.make_async_remote_copy(
-            src_ref=sent.at[source],
+            src_ref=sent.at[source, pl.ds(0, columns)],
             dst_ref=out_ref.at[
                 pl.ds(pl.multiple_of(piece * PIECE, PIECE), PIECE),
-                pl.ds(pl.multiple_of(me * width, width), width),
+                pl.ds(pl.multiple_of(me * width, width), columns),
             ],
             send_sem=send_sem.at[link, piece],
             recv_sem=recv_sem.at[link, piece],
@@ -128,35 +150,107 @@
             device_id_type=MESH,
         )
 
-    def attend(first, key_first, blocks):
-        keys = blocks * BLK
+    def value_copy(step):
+        partner = device(target(step))
+        link = xor(me, partner) - 1
+        rows = keys_of(PACKED - 1)
+        return pltpu.make_async_remote_copy(
+            src_ref=v_ref.at[pl.ds(pl.multiple_of(partner * chunk, chunk), rows)],
+            dst_ref=v_came.at[link],
+            send_sem=v_send_sem.at[link],
+            recv_sem=v_recv_sem.at[link],
+            device_id={"head": partner},
+            device_id_type=MESH,
+        )
+
+    def each_form(is_narrow, piece, act):
+        for number in range(PACKED):
+
+            @pl.when((is_narrow == 1) & (piece == number))
+            def _(number=number):
+                act(keys_of(number) * GROUP, number)
+
+        @pl.when((is_narrow == 0) | (piece >= PACKED))
+        def _():
+            act(width, None)
+
+    def weigh(first, key_first, keys):
         rows = pl.ds(first, PIECE)
-        window = pl.ds(key_first, keys)
         queries = jnp.concatenate(
             [q_ref[rows, g * WIDTH : (g + 1) * WIDTH] for g in range(GROUP)], axis=0
         )
         scores = lax.dot_general(
-            queries, k_ref[window, :], (((1,), (1,)), ((), ())),
+            queries, k_ref[pl.ds(key_first, keys), :], (((1,), (1,)), ((), ())),
             preferred_element_type=jnp.float32,
         )
         own = seg_col[rows, :]
         own = jnp.concatenate([own] * (keys // 128), axis=1)
-        key_seg = seg_ref[0:1, window]
+        key_seg = seg_ref[0:1, pl.ds(key_first, keys)]
         key_at = key_first + lax.broadcasted_iota(jnp.int32, (PIECE, keys), 1)
         own_at = first + lax.broadcasted_iota(jnp.int32, (PIECE, keys), 0)
         allowed = (own == key_seg) & (key_at <= own_at)
         bias = jnp.where(allowed, 0.0, -jnp.inf)
         scores = scores.reshape(GROUP, PIECE, keys) + bias[None]
         row_max = jnp.max(scores, axis=-1, keepdims=True)
-        weights = jnp.exp2((scores - row_max) * scale)
+        return jnp.exp2((scores - row_max) * scale)
+
+    def attend(first, key_first, blocks):
+        keys = blocks * BLK
+        weights = weigh(first, key_first, keys)
         total = jnp.sum(weights, axis=-1, keepdims=True)
         mixed = jnp.dot(
-            weights.astype(jnp.bfloat16).reshape(GROUP * PIECE, keys), v_ref[window, :],
+            weights.astype(jnp.bfloat16).reshape(GROUP * PIECE, keys),
+            v_ref[pl.ds(key_first, keys), :],
             preferred_element_type=jnp.float32,
         )
         mixed = mixed.reshape(GROUP, PIECE, WIDTH) / total
         for g in range(GROUP):
-            sent[rows, g * WIDTH : (g + 1) * WIDTH] = mixed[g].astype(jnp.bfloat16)
+            sent[pl.ds(first, PIECE), g * WIDTH : (g + 1) * WIDTH] = mixed[g].astype(jnp.bfloat16)
+
+    def pack(first, key_first, number):
+        weights = weigh(first, key_first, chunk).astype(jnp.bfloat16)
+        together, keys = TOGETHER[number], keys_of(number)
+        for start in range(0, GROUP, together):
+            wide = jnp.concatenate([weights[start + g] for g in range(together)], axis=1)
+            dense = lax.dot_general(
+                wide, spread[number][...], (((1,), (1,)), ((), ())),
+                preferred_element_type=jnp.float32,
+            )
+            sent[pl.ds(first, PIECE), start * keys : (start + together) * keys] = dense.astype(
+                jnp.bfloat16
+            )
+
+    def expand(source, link):
+        at = pl.multiple_of(source * width, width)
+        came = v_came[link]
+        came = jnp.concatenate(
+            [came, jnp.zeros((WIDTH - came.shape[0], WIDTH), came.dtype)], axis=0
+        )
+        done = []
+        for number in range(PACKED):
+            together, keys = TOGETHER[number], keys_of(number)
+            rows = pl.ds(number * PIECE, PIECE)
+            wide = [
+                jnp.dot(
+                    out_ref[rows, pl.ds(pl.multiple_of(at + start * keys, 128), together * keys)],
+                    spread[number][...], preferred_element_type=jnp.float32,
+                )
+                for start in range(0, GROUP, together)
+            ]
+            weights = jnp.concatenate(
+                [w[:, g * WIDTH : (g + 1) * WIDTH] for w in wide for g in range(together)], axis=0
+            )
+            total = jnp.sum(weights, axis=-1, keepdims=True)
+            mixed = jnp.dot(
+                weights.astype(jnp.bfloat16), came, preferred_element_type=jnp.float32
+            )
+            done.append((mixed * (1.0 / total)).astype(jnp.bfloat16))
+        for number in range(PACKED):
+            for g in range(GROUP):
+                out_ref[
+                    number * PIECE : (number + 1) * PIECE,
+                    pl.ds(pl.multiple_of(at + g * WIDTH, WIDTH), WIDTH),
+                ] = done[number][g * PIECE : (g + 1) * PIECE]
 
     def one_step(step, carry):
         partner = device(target(step))
@@ -166,18 +260,31 @@
         blocks = light + (1 - light) * (block + 1)
         key_first = pl.multiple_of(light * block * BLK, BLK)
 
+        away = 1 - step // (HEADS - 1)
+        is_narrow = narrow(partner) * away
+
+        @pl.when(is_narrow == 1)
+        def _():
+            value_copy(step).start()
+
         def one_piece(piece, inner):
             first = pl.multiple_of(partner * chunk + piece * PIECE, PIECE)
-            for count in range(1, tokens // BLK + 1):
-
-                @pl.when(blocks == count)
-                def _(count=count):
-                    attend(first, key_first if count == 1 else 0, count)
-
-            @pl.when(step < HEADS - 1)
-            def _():
-                piece_copy(step, piece).start()
-
+
+            def form(columns, number):
+                if number is None:
+                    for count in range(1, tokens // BLK + 1):
+
+                        @pl.when(blocks == count)
+                        def _(count=count):
+                            attend(first, key_first if count == 1 else 0, count)
+                else:
+                    pack(first, key_first, number)
+
+                @pl.when(away == 1)
+                def _():
+                    piece_copy(step, piece, columns).start()
+
+            each_form(is_narrow, piece, form)
             return inner
 
         return lax.fori_loop(0, pieces, one_piece, carry)
@@ -192,16 +299,48 @@
     home.start()
     home.wait()
 
-    def finish(step, carry):
+    def unpack(place_in_order, carry):
+        near = place_in_order // half
+        step = (1 - near) * (place_in_order * 2 - (place_in_order + 3) // half) + near * 2 * (
+            place_in_order - half + 1
+        )
+        partner = device(target(step))
+        value_copy(step).wait_recv()
+        for number in range(PACKED):
+            piece_copy(step, number, keys_of(number) * GROUP).wait_recv()
+        expand(partner, xor(me, partner) - 1)
+        return carry
+
+    @pl.when(narrow(me) == 1)
+    def _():
+        lax.fori_loop(0, HEADS - 1, unpack, 0)
+
+    def arrive(step, carry):
         def one_piece(piece, inner):
-            copy = piece_copy(step, piece)
-            copy.wait_send()
-            copy.wait_recv()
+            piece_copy(step, piece, width).wait_recv()
             return inner
 
+        return lax.fori_loop(narrow(me) * PACKED, pieces, one_piece, carry)
+
+    lax.fori_loop(0, HEADS - 1, arrive, 0)
+
+    def leave(step, carry):
+        is_narrow = narrow(device(target(step)))
+
+        @pl.when(is_narrow == 1)
+        def _():
+            value_copy(step).wait_send()
+
+        def one_piece(piece, inner):
+            def form(columns, number):
+                piece_copy(step, piece, columns).wait_send()
+
+            each_form(is_narrow, piece, form)
+            return inner
+
         return lax.fori_loop(0, pieces, one_piece, carry)
 
-    lax.fori_loop(0, HEADS - 1, finish, 0)
+    lax.fori_loop(0, HEADS - 1, leave, 0)
 
 
 def on_device(queries, keys, values, segments):
@@ -220,10 +359,17 @@
             pltpu.VMEM(segments.shape, segments.dtype),
             pltpu.VMEM((tokens, 128), jnp.int32),
             pltpu.VMEM(queries.shape, queries.dtype),
+            pltpu.VMEM((HEADS - 1, keys_of(PACKED - 1), WIDTH), values.dtype),
+            *[
+                pltpu.VMEM((TOGETHER[p] * keys_of(p), TOGETHER[p] * WIDTH), queries.dtype)
+                for p in range(PACKED)
+            ],
             pltpu.SemaphoreType.DMA((HEADS,)),
             pltpu.SemaphoreType.DMA((3,)),
             pltpu.SemaphoreType.DMA((HEADS - 1, pieces)),
             pltpu.SemaphoreType.DMA((HEADS - 1, pieces)),
+            pltpu.SemaphoreType.DMA((HEADS - 1,)),
+            pltpu.SemaphoreType.DMA((HEADS - 1,)),
             pltpu.SemaphoreType.REGULAR((HEADS // 2,)),
         ],
         compiler_params=pltpu.CompilerParams(

time: 102 us -> 97.1 us (0.952)
  the two profiles are of different devices: /device:TPU:275 before, /device:TPU:414 now
where the time goes in v2:
time: 97.1 us; the launch traced here: 96.9 us
  Pallas kernels  95.6 us (98%)
  local copies, waits for them, and re-layouts  1.32 us (1%)
    pallas_call x1, Pallas kernels, on_device(): pl.pallas_call(kernel, out_shape=pltpu.VMEM((chunk, HEADS * width), queri...  95.6 us

profile of v2, /device:TPU:414, one launch (start us, length us, event | category | flops | bytes accessed | tf_op | source)
XLA Modules:
  0.0 96.9 jit_solution(3560950168523661368)
XLA Ops:
  0.0 95.6 %shard_map.46 = bf16[128,8192]{1,0:T(8,128)(2,1)S(1)} custom-call(bf16[1024,1024]{1,0:T(8,128)(2,1)} %q_hbm.1, bf16[1024,128]{1,0:T(8,128)(2,1)} %k_hbm.1, bf16[1024,128]{1,0:T(8,128)(2,1)} %v_hbm.1, s32[1,1024]{1,0:T(1,128)} %seg_hbm.1), custom_call_target="tpu_custom_call" | custom-call | flops 4294967296 | bytes 5242880 | tf_op jit(solution)/shard_map/pallas_call | solution.py:350
  95.6 1.3 %copy.6 = bf16[128,8192]{1,0:T(8,128)(2,1)} copy(bf16[128,8192]{1,0:T(8,128)(2,1)S(1)} %shard_map.46) | data formatting | bytes 4194304

commit v3 on v2

--- a/solution.py
+++ b/solution.py
@@ -13,6 +13,9 @@
 MESH = pl.DeviceIdType.MESH
 LOG2E = 1.4426950408889634
 PACKED = 3
+ORDER = (0, -3, 1, -2, 2, -1, 3)
+EARLY = ((0, 3, 2, 1), (3, 2, 1, 0))
+FIRST_NEAR = min(step for step, turn in enumerate(ORDER) if turn < 0)
 TOGETHER = (4, 2, 4)
 
 
@@ -20,17 +23,17 @@
     return (piece + 1) * PIECE
 
 
-def xor(a, b):
-    total = 0
-    for bit in (1, 2, 4):
-        total = total + bit * (((a // bit) % 2 + (b // bit) % 2) % 2)
-    return total
+def pick(step, values):
+    chosen = values[-1]
+    for at in range(len(values) - 2, -1, -1):
+        chosen = jnp.where(step == at, values[at], chosen)
+    return chosen
 
 
 def kernel(
     q_hbm, k_hbm, v_hbm, seg_hbm, out_ref,
     q_ref, k_ref, v_ref, seg_ref, seg_col, sent, v_came, spread_0, spread_1, spread_2,
-    q_sem, in_sem, send_sem, recv_sem, v_send_sem, v_recv_sem, ready,
+    q_sem, in_sem, send_sem, wide_sem, packed_sem, ready,
 ):
     tokens, width = q_ref.shape
     chunk = tokens // HEADS
@@ -40,33 +43,47 @@
     scale = WIDTH**-0.5 * LOG2E
     me = lax.axis_index("head")
     replica = lax.axis_index("dp")
+    replicas = lax.axis_size("dp")
     ones = 0
-    for bit in range(16):
-        ones = ones + (replica // 2**bit) % 2
-    light = ones % 2
+    for bit in range((replicas - 1).bit_length()):
+        ones = ones + lax.rem(lax.div(replica, 2**bit), 2)
+    light = lax.rem(ones, 2)
 
     def narrow(at):
-        even = 1 - at % (BLK // chunk)
-        first = 1 - (at + HEADS - 1) // HEADS
+        even = 1 - lax.rem(at, BLK // chunk)
+        first = 1 - lax.div(at + HEADS - 1, HEADS)
         return light * even + (1 - light) * first
 
-    flip = replica // (lax.axis_size("dp") // 2)
+    flip = lax.div(replica, replicas // 2)
     place = me + flip * (HEADS - 1 - 2 * me)
-    late = place // half
+    late = lax.div(place, half)
+    within = place - half * late
+    low = lax.rem(within, 2)
+    high = lax.div(within, 2)
+
+    def mixed_with(i):
+        return (1 - low if i % 2 else low) + 2 * (1 - high if i // 2 else high)
 
     def device(at):
         return at + flip * (HEADS - 1 - 2 * at)
 
-    def target(step):
-        last = step // (HEADS - 1)
-        odd = (step % 2) * (1 - last)
-        across = odd + 1 - (step + HEADS - 2) // (HEADS - 1)
-        other = (step + 1) // 2 + half * (1 - late)
-        near = half * late + xor(place % half, (step // 2) * (1 - last))
-        return across * other + (1 - across) * near
-
-    def q_copy(step):
-        rows = pl.ds(pl.multiple_of(device(target(step)) * chunk, chunk), chunk)
+    kind = (1 - late) * (1 + flip)
+    partners, links = [], []
+    for turn in ORDER:
+        if turn >= 0:
+            orders = (turn, EARLY[0][turn], EARLY[1][turn])
+            partners.append(device(pick(kind, orders) + half * (1 - late)))
+            links.append(half - 1 + pick(kind, [mixed_with(at) for at in orders]))
+        else:
+            partners.append(device(half * late + mixed_with(-turn)))
+            links.append(-turn - 1)
+    partners.append(me)
+    links.append(0)
+    narrows = [narrow(at) for at in partners]
+    narrow_here = narrow(me)
+
+    def q_copy(step, partner):
+        rows = pl.ds(pl.multiple_of(partner * chunk, chunk), chunk)
         return pltpu.make_async_copy(q_hbm.at[rows], q_ref.at[rows], q_sem.at[step])
 
     def greet(at, semaphore):
@@ -90,11 +107,11 @@
     k_copy = pltpu.make_async_copy(k_hbm, k_ref, in_sem.at[0])
     v_copy = pltpu.make_async_copy(v_hbm, v_ref, in_sem.at[1])
     seg_copy.start()
-    q_copy(0).start()
+    q_copy(0, partners[0]).start()
     k_copy.start()
     v_copy.start()
     for step in range(1, HEADS):
-        q_copy(step).start()
+        q_copy(step, partners[step]).start()
     seg_copy.wait()
     for part in range(tokens // 128):
         row = seg_ref[0:1, part * 128 : (part + 1) * 128]
@@ -121,22 +138,21 @@
             greet(at, ready.at[place - half])
 
     def admit(step):
-        @pl.when(step == 2)
-        def _():
-            pl.semaphore_wait(ready.at[0], 1)
-
-        @pl.when((late == 0) & (step % 2 == 1) & (step < HEADS - 1))
-        def _():
-            pl.semaphore_wait(ready.at[(step + 1) // 2], 1)
-
-        @pl.when((place == half - 1) & (step == HEADS - 3))
+        @pl.when((late == 0) & (step == 1 - flip))
+        def _():
+            for at in range(half):
+                pl.semaphore_wait(ready.at[at], 1)
+
+        @pl.when((place == half - 1) & (step == 1 - flip))
         def _():
             for at in range(half, HEADS):
                 greet(at, ready.at[0])
 
-    def piece_copy(step, piece, columns):
-        partner = device(target(step))
-        link = xor(me, partner) - 1
+        @pl.when((late == 1) & (step == FIRST_NEAR))
+        def _():
+            pl.semaphore_wait(ready.at[0], 1)
+
+    def piece_copy(partner, link, piece, columns, came):
         source = pl.ds(pl.multiple_of(partner * chunk + piece * PIECE, PIECE), PIECE)
         return pltpu.make_async_remote_copy(
             src_ref=sent.at[source, pl.ds(0, columns)],
@@ -144,24 +160,25 @@
                 pl.ds(pl.multiple_of(piece * PIECE, PIECE), PIECE),
                 pl.ds(pl.multiple_of(me * width, width), columns),
             ],
-            send_sem=send_sem.at[link, piece],
-            recv_sem=recv_sem.at[link, piece],
+            send_sem=send_sem.at[link],
+            recv_sem=came,
             device_id={"head": partner},
             device_id_type=MESH,
         )
 
-    def value_copy(step):
-        partner = device(target(step))
-        link = xor(me, partner) - 1
+    def value_copy(partner, link):
         rows = keys_of(PACKED - 1)
         return pltpu.make_async_remote_copy(
             src_ref=v_ref.at[pl.ds(pl.multiple_of(partner * chunk, chunk), rows)],
             dst_ref=v_came.at[link],
-            send_sem=v_send_sem.at[link],
-            recv_sem=v_recv_sem.at[link],
+            send_sem=send_sem.at[link],
+            recv_sem=packed_sem.at[link],
             device_id={"head": partner},
             device_id_type=MESH,
         )
+
+    def wait_bytes(semaphore, ref):
+        pltpu.make_async_copy(ref, ref, semaphore).wait()
 
     def each_form(is_narrow, piece, act):
         for number in range(PACKED):
@@ -253,19 +270,17 @@
                 ] = done[number][g * PIECE : (g + 1) * PIECE]
 
     def one_step(step, carry):
-        partner = device(target(step))
-        q_copy(step).wait()
+        partner, link = pick(step, partners), pick(step, links)
+        q_copy(step, partner).wait()
         admit(step)
-        block = partner // (BLK // chunk)
+        block = lax.div(partner, BLK // chunk)
         blocks = light + (1 - light) * (block + 1)
         key_first = pl.multiple_of(light * block * BLK, BLK)
-
-        away = 1 - step // (HEADS - 1)
-        is_narrow = narrow(partner) * away
+        is_narrow = pick(step, narrows[:-1] + [0])
 
         @pl.when(is_narrow == 1)
         def _():
-            value_copy(step).start()
+            value_copy(partner, link).start()
 
         def one_piece(piece, inner):
             first = pl.multiple_of(partner * chunk + piece * PIECE, PIECE)
@@ -280,9 +295,10 @@
                 else:
                     pack(first, key_first, number)
 
-                @pl.when(away == 1)
+                @pl.when(step < HEADS - 1)
                 def _():
-                    piece_copy(step, piece, columns).start()
+                    came = wide_sem.at[0] if number is None else packed_sem.at[link]
+                    piece_copy(partner, link, piece, columns, came).start()
 
             each_form(is_narrow, piece, form)
             return inner
@@ -299,54 +315,45 @@
     home.start()
     home.wait()
 
-    def unpack(place_in_order, carry):
-        near = place_in_order // half
-        step = (1 - near) * (place_in_order * 2 - (place_in_order + 3) // half) + near * 2 * (
-            place_in_order - half + 1
-        )
-        partner = device(target(step))
-        value_copy(step).wait_recv()
-        for number in range(PACKED):
-            piece_copy(step, number, keys_of(number) * GROUP).wait_recv()
-        expand(partner, xor(me, partner) - 1)
+    weight_rows = sum(keys_of(p) * GROUP * PIECE for p in range(PACKED)) // WIDTH
+    packed_rows = weight_rows + keys_of(PACKED - 1)
+    wide_rows = PIECE * width // WIDTH
+
+    def unpack(at, carry):
+        link = pick(at, links)
+        wait_bytes(packed_sem.at[link], k_ref.at[pl.ds(0, packed_rows)])
+        expand(pick(at, partners), link)
         return carry
 
-    @pl.when(narrow(me) == 1)
+    @pl.when(narrow_here == 1)
     def _():
         lax.fori_loop(0, HEADS - 1, unpack, 0)
 
-    def arrive(step, carry):
-        def one_piece(piece, inner):
-            piece_copy(step, piece, width).wait_recv()
-            return inner
-
-        return lax.fori_loop(narrow(me) * PACKED, pieces, one_piece, carry)
-
-    lax.fori_loop(0, HEADS - 1, arrive, 0)
-
-    def leave(step, carry):
-        is_narrow = narrow(device(target(step)))
-
-        @pl.when(is_narrow == 1)
-        def _():
-            value_copy(step).wait_send()
-
-        def one_piece(piece, inner):
-            def form(columns, number):
-                piece_copy(step, piece, columns).wait_send()
-
-            each_form(is_narrow, piece, form)
-            return inner
-
-        return lax.fori_loop(0, pieces, one_piece, carry)
-
-    lax.fori_loop(0, HEADS - 1, leave, 0)
+    for step in range(HEADS - 1):
+
+        @pl.when(narrows[step] == 1)
+        def _(step=step):
+            left = packed_rows + (pieces - PACKED) * wide_rows
+            wait_bytes(send_sem.at[links[step]], k_ref.at[pl.ds(0, left)])
+
+        @pl.when(narrows[step] == 0)
+        def _(step=step):
+            wait_bytes(send_sem.at[links[step]], k_ref.at[pl.ds(0, pieces * wide_rows)])
+
+    others = pl.ds(0, (HEADS - 1) * width)
+
+    @pl.when(narrow_here == 1)
+    def _():
+        wait_bytes(wide_sem.at[0], out_ref.at[pl.ds(0, (pieces - PACKED) * PIECE), others])
+
+    @pl.when(narrow_here == 0)
+    def _():
+        wait_bytes(wide_sem.at[0], out_ref.at[:, others])
 
 
 def on_device(queries, keys, values, segments):
     tokens, width = queries.shape
     chunk = tokens // HEADS
-    pieces = chunk // PIECE
     return pl.pallas_call(
         kernel,
         out_shape=pltpu.VMEM((chunk, HEADS * width), queries.dtype),
@@ -366,9 +373,8 @@
             ],
             pltpu.SemaphoreType.DMA((HEADS,)),
             pltpu.SemaphoreType.DMA((3,)),
-            pltpu.SemaphoreType.DMA((HEADS - 1, pieces)),
-            pltpu.SemaphoreType.DMA((HEADS - 1, pieces)),
             pltpu.SemaphoreType.DMA((HEADS - 1,)),
+            pltpu.SemaphoreType.DMA((1,)),
             pltpu.SemaphoreType.DMA((HEADS - 1,)),
             pltpu.SemaphoreType.REGULAR((HEADS // 2,)),
         ],

time: 97.1 us -> 93 us (0.958)
  the two profiles are of different devices: /device:TPU:414 before, /device:TPU:189 now
where the time goes in v3:
time: 93 us; the launch traced here: 92.9 us
  Pallas kernels  91.5 us (98%)
  local copies, waits for them, and re-layouts  1.32 us (1%)
    pallas_call x1, Pallas kernels, on_device(): pl.pallas_call(kernel, out_shape=pltpu.VMEM((chunk, HEADS * width), queri...  91.5 us

profile of v3, /device:TPU:189, one launch (start us, length us, event | category | flops | bytes accessed | tf_op | source)
XLA Modules:
  0.0 92.9 jit_solution(14433435134311160326)
XLA Ops:
  0.0 91.5 %shard_map.46 = bf16[128,8192]{1,0:T(8,128)(2,1)S(1)} custom-call(bf16[1024,1024]{1,0:T(8,128)(2,1)} %q_hbm.1, bf16[1024,128]{1,0:T(8,128)(2,1)} %k_hbm.1, bf16[1024,128]{1,0:T(8,128)(2,1)} %v_hbm.1, s32[1,1024]{1,0:T(1,128)} %seg_hbm.1), custom_call_target="tpu_custom_call" | custom-call | flops 4294967296 | bytes 5242880 | tf_op jit(solution)/shard_map/pallas_call | solution.py:357
  91.5 1.3 %copy.6 = bf16[128,8192]{1,0:T(8,128)(2,1)} copy(bf16[128,8192]{1,0:T(8,128)(2,1)S(1)} %shard_map.46) | data formatting | bytes 4194304

commit v4 on v3

--- a/solution.py
+++ b/solution.py
@@ -112,6 +112,12 @@
     v_copy.start()
     for step in range(1, HEADS):
         q_copy(step, partners[step]).start()
+    @pl.when(late == 1)
+    def _():
+        pl.semaphore_wait(barrier, half)
+        for at in range(half):
+            greet(at, ready.at[place - half])
+
     seg_copy.wait()
     for part in range(tokens // 128):
         row = seg_ref[0:1, part * 128 : (part + 1) * 128]
@@ -127,17 +133,11 @@
     k_copy.wait()
     v_copy.wait()
 
-    @pl.when(late == 0)
-    def _():
-        pl.semaphore_wait(barrier, 1)
-
-    @pl.when(late == 1)
-    def _():
-        pl.semaphore_wait(barrier, half)
-        for at in range(half):
-            greet(at, ready.at[place - half])
-
     def admit(step):
+        @pl.when((late == 0) & (step == 0))
+        def _():
+            pl.semaphore_wait(barrier, 1)
+
         @pl.when((late == 0) & (step == 1 - flip))
         def _():
             for at in range(half):
@@ -272,15 +272,10 @@
     def one_step(step, carry):
         partner, link = pick(step, partners), pick(step, links)
         q_copy(step, partner).wait()
-        admit(step)
         block = lax.div(partner, BLK // chunk)
         blocks = light + (1 - light) * (block + 1)
         key_first = pl.multiple_of(light * block * BLK, BLK)
         is_narrow = pick(step, narrows[:-1] + [0])
-
-        @pl.when(is_narrow == 1)
-        def _():
-            value_copy(partner, link).start()
 
         def one_piece(piece, inner):
             first = pl.multiple_of(partner * chunk + piece * PIECE, PIECE)
@@ -294,6 +289,12 @@
                             attend(first, key_first if count == 1 else 0, count)
                 else:
                     pack(first, key_first, number)
+
+                @pl.when(piece == 0)
+                def _():
+                    admit(step)
+                    if number == 0:
+                        value_copy(partner, link).start()
 
                 @pl.when(step < HEADS - 1)
                 def _():

time: 93 us -> 92.3 us (level)
  the two profiles are of different devices: /device:TPU:189 before, /device:TPU:414 now
where the time goes in v4:
time: 92.3 us; the launch traced here: 91.5 us
  Pallas kernels  90.2 us (98%)
  local copies, waits for them, and re-layouts  1.32 us (1%)
    pallas_call x1, Pallas kernels, on_device(): pl.pallas_call(kernel, out_shape=pltpu.VMEM((chunk, HEADS * width), queri...  90.2 us

profile of v4, /device:TPU:414, one launch (start us, length us, event | category | flops | bytes accessed | tf_op | source)
XLA Modules:
  0.0 91.5 jit_solution(15225602437349908064)
XLA Ops:
  0.0 90.2 %shard_map.46 = bf16[128,8192]{1,0:T(8,128)(2,1)S(1)} custom-call(bf16[1024,1024]{1,0:T(8,128)(2,1)} %q_hbm.1, bf16[1024,128]{1,0:T(8,128)(2,1)} %k_hbm.1, bf16[1024,128]{1,0:T(8,128)(2,1)} %v_hbm.1, s32[1,1024]{1,0:T(1,128)} %seg_hbm.1), custom_call_target="tpu_custom_call" | custom-call | flops 4294967296 | bytes 5242880 | tf_op jit(solution)/shard_map/pallas_call | solution.py:358
  90.2 1.3 %copy.6 = bf16[128,8192]{1,0:T(8,128)(2,1)} copy(bf16[128,8192]{1,0:T(8,128)(2,1)S(1)} %shard_map.46) | data formatting | bytes 4194304

commit v5 on v4

--- a/solution.py
+++ b/solution.py
@@ -13,7 +13,7 @@
 MESH = pl.DeviceIdType.MESH
 LOG2E = 1.4426950408889634
 PACKED = 3
-ORDER = (0, -3, 1, -2, 2, -1, 3)
+ORDER = (0, -3, 1, -2, 2, 3, -1)
 EARLY = ((0, 3, 2, 1), (3, 2, 1, 0))
 FIRST_NEAR = min(step for step, turn in enumerate(ORDER) if turn < 0)
 TOGETHER = (4, 2, 4)

time: 92.3 us -> 92.3 us (level)
  the two profiles are of different devices: /device:TPU:414 before, /device:TPU:409 now
where the time goes in v5:
time: 92.3 us; the launch traced here: 92.2 us
  Pallas kernels  90.9 us (98%)
  local copies, waits for them, and re-layouts  1.32 us (1%)
    pallas_call x1, Pallas kernels, on_device(): pl.pallas_call(kernel, out_shape=pltpu.VMEM((chunk, HEADS * width), queri...  90.9 us

profile of v5, /device:TPU:409, one launch (start us, length us, event | category | flops | bytes accessed | tf_op | source)
XLA Modules:
  0.0 92.2 jit_solution(14628956662903358778)
XLA Ops:
  0.0 90.9 %shard_map.46 = bf16[128,8192]{1,0:T(8,128)(2,1)S(1)} custom-call(bf16[1024,1024]{1,0:T(8,128)(2,1)} %q_hbm.1, bf16[1024,128]{1,0:T(8,128)(2,1)} %k_hbm.1, bf16[1024,128]{1,0:T(8,128)(2,1)} %v_hbm.1, s32[1,1024]{1,0:T(1,128)} %seg_hbm.1), custom_call_target="tpu_custom_call" | custom-call | flops 4294967296 | bytes 5242880 | tf_op jit(solution)/shard_map/pallas_call | solution.py:358
  90.9 1.3 %copy.6 = bf16[128,8192]{1,0:T(8,128)(2,1)} copy(bf16[128,8192]{1,0:T(8,128)(2,1)S(1)} %shard_map.46) | data formatting | bytes 4194304
